TPU v7x, 32 devices: a whole 2x2x4 slice. The times are simulated.
32 devices in a mesh: grp: 2 (over y), gx: 4 (over z), gy: 2 (over x), hour: 2 (over core).
Axes of the slice: x: 2, y: 2, z: 4, core: 2. Of those that a mesh axis runs over, the one named last changes fastest.
Arguments:
- control: float32 [32, 512, 1024], P(('grp', 'hour'), 'gx', 'gy'), parts along dimension 0, may hold values from -6 to 6
- background_scale: bfloat16 [32, 512, 1024], P(('grp', 'hour'), 'gx', 'gy'), parts along dimension 0, may hold values from 0.29882812 to 3
- rate_x: float32 [32, 512], P(('grp', 'hour'), 'gx'), parts along dimension 0, as said below
- rate_y: float32 [32, 1024], P(('grp', 'hour')), parts along dimension 0, as said below
- obs_owner: int32 [4096], P(('grp', 'gx', 'gy')), parts along dimension 0, may hold values from 0 to 7, as said below
- stencil: int32 [4096, 16], P(('grp', 'gx', 'gy')), parts along dimension 0, may hold values from 0 to 65535, as said below
- obs_weights: float32 [4096, 256], P(('grp', 'gx', 'gy'), 'hour'), parts along dimension 0, may hold values from -0.375 to 0.375
- innovation: float32 [4096], P(('grp', 'gx', 'gy')), parts along dimension 0, may hold values from -6 to 6
- obs_sigma: float32 [4096], P(('grp', 'gx', 'gy')), parts along dimension 0, may hold values from 0.3 to 3
Outputs:
- increment: float32 [32, 512, 1024], P(('grp', 'hour'), 'gx', 'gy'), parts along dimension 0
- departure: float32 [4096], P(('grp', 'gx', 'gy')), parts along dimension 0
There are 2 independent parts, one for each index of `grp`. A program takes and returns all parts, laid end to end along the dimension named above; each array names one. Nothing has to cross between parts.
Inputs may be any that keep to these rules, and one draw needn't show every extreme that they name: `obs_owner`: each value is an owner index over gx+gy in mesh order. At most 64 of the observations of one device go to one owner, and in every draw one owner receives exactly 64 from every device. `stencil`: the 16 cells of an observation form a 4 by 4 block of its owner's tile of 128 by 512 cells. `rate_x`: Positive. `rate_y`: Positive.
All inputs are finite; a program needn't handle non-finite values.
Results may differ from a plain program's by a relative error of at most 0.0003.
Values sent between devices are 32-bit elements; how exact they have to be, the bound alone decides.
A program may use at most 128 MiB of HBM per device.

v0:
```python
import jax
import jax.numpy as jnp
from jax import lax
from jax.sharding import PartitionSpec as P

EXACT = lax.Precision.HIGHEST


def prefix(part, axis, combine, identity, reverse):
    count = lax.axis_size(axis)
    place = lax.axis_index(axis)
    ahead = count - 1 - place if reverse else place
    gathered = jax.tree.map(lambda a: lax.all_gather(a, axis), part)
    state = jax.tree.map(lambda a, e: jnp.zeros_like(a) + jnp.asarray(e, a.dtype), part, identity)

    def one(hop, state):
        source = count - 1 - hop if reverse else hop
        return combine(
            state, jax.tree.map(lambda a: lax.dynamic_index_in_dim(a, source, 0, False), gathered)
        )

    return lax.fori_loop(0, ahead, one, state)


def forward_table(rate_slice, running):
    length = rate_slice.shape[1]
    row_index = lax.broadcasted_iota(jnp.int32, (length, length), 0)
    col_index = lax.broadcasted_iota(jnp.int32, (length, length), 1)
    lower_part = (row_index >= col_index)[None]
    spread = jnp.where(lower_part, running[:, :, None] - running[:, None, :], 0.0)
    gains = jnp.sqrt(-jnp.expm1(-2.0 * rate_slice))
    matrix = jnp.where(lower_part, jnp.exp(-spread), 0.0) * gains[:, None, :]
    return (matrix, jnp.exp(-running))


def backward_table(rate_slice, running):
    length = rate_slice.shape[1]
    before = running - rate_slice
    row_index = lax.broadcasted_iota(jnp.int32, (length, length), 0)
    col_index = lax.broadcasted_iota(jnp.int32, (length, length), 1)
    upper_part = (col_index >= row_index)[None]
    spread = jnp.where(upper_part, before[:, None, :] - before[:, :, None], 0.0)
    gains = -jnp.expm1(-rate_slice)
    matrix = jnp.where(upper_part, jnp.exp(-spread), 0.0) * gains[:, None, :]
    return (matrix, jnp.exp(-(running[:, -1:] - before)))


def compose(farther, nearer):
    return (farther[0] * nearer[0], nearer[0][:, None] * farther[1] + nearer[1])


def filter_x(control, rate_x):
    running = jnp.cumsum(rate_x, axis=1)
    matrix, lead_factor = forward_table(rate_x, running)
    overall = lead_factor[:, -1]
    inside = jnp.einsum("lij,ljy->liy", matrix, control, precision=EXACT)
    neutral = (jnp.ones_like(overall), jnp.zeros_like(inside[:, 0, :]))
    entering = prefix((overall, inside[:, -1, :]), "gx", compose, neutral, False)[1]
    smooth = inside + lead_factor[:, :, None] * entering[:, None, :]
    matrix, trail_factor = backward_table(rate_x, running)
    inside = jnp.einsum("lij,ljy->liy", matrix, smooth, precision=EXACT)
    entering = prefix((overall, inside[:, 0, :]), "gx", compose, neutral, True)[1]
    return inside + trail_factor[:, :, None] * entering[:, None, :]


def filter_y(along_x, rate_y):
    block_width = along_x.shape[2]
    rate_slice = lax.dynamic_slice_in_dim(
        rate_y, lax.axis_index("gy") * block_width, block_width, 1
    )
    running = jnp.cumsum(rate_slice, axis=1)
    matrix, lead_factor = forward_table(rate_slice, running)
    overall = lead_factor[:, -1]
    inside = jnp.einsum("lij,lxj->lxi", matrix, along_x, precision=EXACT)
    neutral = (jnp.ones_like(overall), jnp.zeros_like(inside[:, :, 0]))
    entering = prefix((overall, inside[:, :, -1]), "gy", compose, neutral, False)[1]
    smooth = inside + entering[:, :, None] * lead_factor[:, None, :]
    matrix, trail_factor = backward_table(rate_slice, running)
    inside = jnp.einsum("lij,lxj->lxi", matrix, smooth, precision=EXACT)
    entering = prefix((overall, inside[:, :, 0]), "gy", compose, neutral, True)[1]
    return inside + entering[:, :, None] * trail_factor[:, None, :]


def observe(increment, obs_owner, stencil, obs_weights, innovation, obs_sigma):
    across = lax.axis_size("gx")
    along_y_count = lax.axis_size("gy")
    owners = across * along_y_count
    obs_count = obs_owner.shape[0]
    capacity = 2 * obs_count // owners
    levels = increment.shape[0]
    points = stencil.shape[1]
    row_index = lax.broadcasted_iota(jnp.int32, (obs_count, obs_count), 0)
    col_index = lax.broadcasted_iota(jnp.int32, (obs_count, obs_count), 1)
    matching = (obs_owner[:, None] == obs_owner[None, :]) & (col_index < row_index)
    position = jnp.sum(matching.astype(jnp.int32), axis=1)
    target = obs_owner * capacity + position
    send_weights = (
        jnp.zeros((owners * capacity, obs_weights.shape[1]), jnp.float32)
        .at[target]
        .set(obs_weights)
    )
    send_cells = jnp.zeros((owners * capacity, points), jnp.int32).at[target].set(stencil)
    flattened = increment.reshape(levels, -1)
    weights_in = lax.all_to_all(
        send_weights.reshape(owners, capacity, -1),
        ("gx", "gy"),
        split_axis=0,
        concat_axis=0,
        tiled=True,
    )
    cells_in = lax.all_to_all(
        send_cells.reshape(owners, capacity, points),
        ("gx", "gy"),
        split_axis=0,
        concat_axis=0,
        tiled=True,
    )
    sources = cells_in.shape[0]
    item_count = cells_in.shape[1]
    slots = sources * item_count
    values = jnp.take(flattened, cells_in.reshape(-1), axis=1).reshape(levels, slots, points)
    shaped = weights_in.reshape(slots, levels, points)
    summed = jnp.sum(jnp.sum(shaped * jnp.swapaxes(values, 0, 1), axis=2), axis=1)
    returned = lax.all_to_all(
        summed.reshape(sources, item_count), ("gx", "gy"), split_axis=0, concat_axis=0, tiled=True
    )
    partial_model = jnp.take(returned.reshape(-1), target)
    modelled = lax.psum(partial_model, "hour")
    return (modelled - innovation) / obs_sigma


def on_device(
    control,
    background_scale,
    rate_x,
    rate_y,
    obs_owner,
    stencil,
    obs_weights,
    innovation,
    obs_sigma,
):
    along_x = filter_x(control, rate_x)
    filtered = filter_y(along_x, rate_y)
    increment = filtered * background_scale.astype(jnp.float32)
    departure = observe(increment, obs_owner, stencil, obs_weights, innovation, obs_sigma)
    return (increment, departure)


def solution(mesh):
    return jax.shard_map(
        on_device,
        mesh=mesh,
        in_specs=(
            P(("grp", "hour"), "gx", "gy"),
            P(("grp", "hour"), "gx", "gy"),
            P(("grp", "hour"), "gx"),
            P(("grp", "hour"), None),
            P(("grp", "gx", "gy")),
            P(("grp", "gx", "gy"), None),
            P(("grp", "gx", "gy"), "hour"),
            P(("grp", "gx", "gy")),
            P(("grp", "gx", "gy")),
        ),
        out_specs=(P(("grp", "hour"), "gx", "gy"), P(("grp", "gx", "gy"))),
        check_vma=False,
    )
```

profile of v0, /device:TPU:0, one launch (start us, length us, event | category | flops | bytes accessed | tf_op | source)
XLA Modules:
  0.0 200.1 jit_solution(15021457396762737596)
XLA Ops:
  5.2 7.3 %all-to-all-start.1 = ((s32[8,1,1024]{2,1,0:T(1,128)}), s32[8,1,1024]{2,1,0:T(1,128)S(1)}, u32[]{:S(2)}, u32[]{:S(2)}) async-start(s32[8,1,1024]{2,1,0:T(1,128)} %reshape.255), calls=%async_computation.1 | async-start | bytes 65536 | tf_op jit(solution)/shard_map/all_to_all | solution.py:111
  20.1 12.2 %all-reduce = f32[32]{0:T(128)S(1)} all-reduce(f32[32]{0:T(128)S(1)} %dynamic-update-slice), channel_id=2, replica_groups=mesh['grp'=2,'gx'=4,'gy'=2,'hour'=2] {'gx'}, use_global_device_ids=true, to_apply=%add | all-reduce | flops 32 | bytes 256
  32.3 2.0 fusion.37
  34.3 1.3 copy-done.1
  35.6 13.1 %all-gather.1 = f32[32,1,512]{2,1,0:T(1,128)S(1)} all-gather(f32[8,1,512]{2,1,0:T(1,128)S(1)} %slice.44), channel_id=3, replica_groups=mesh['grp'=2,'gx'=4,'gy'=2,'hour'=2] {'gx'}, dimensions={0}, use_global_device_ids=true | all-gather | bytes 81920 | tf_op jit(solution)/shard_map/all_gather | solution.py:13
  48.8 3.7 %fusion.28 = f32[8,128,512]{2,1,0:T(8,128)S(1)} fusion(f32[8,128,512]{2,1,0:T(8,128)} %copy-done.1, f32[8,512]{1,0:T(8,128)S(1)} %get-tuple-element.258, f32[8,128]{1,0:T(8,128)S(1)} %get-tuple-element.312, f32[8,128]{1,0:T(8,128)S(1)} %get-tuple-element.311, f32[8,128]{1,0:T(8,128)S(1)} %get-tuple-element.307, pred[128,128]{1,0:T(8,128)(4,1)S(1)} %iota_compare_fusion.4), kind=kOutput, calls=%fused_computation.41 | convolution fusion | flops 807010304 | bytes 4239360 | tf_op jit(solution)/shard_map/lij,ljy->liy/dot_general | solution.py:61
  52.5 1.3 copy-done.3
  53.9 13.1 %all-gather.2 = f32[32,1,512]{2,1,0:T(1,128)S(1)} all-gather(f32[8,1,512]{2,1,0:T(1,128)S(1)} %slice.45), channel_id=4, replica_groups=mesh['grp'=2,'gx'=4,'gy'=2,'hour'=2] {'gx'}, dimensions={0}, use_global_device_ids=true | all-gather | bytes 81920 | tf_op jit(solution)/shard_map/all_gather | solution.py:13
  67.3 12.0 %fusion.7 = f32[8,128,512]{2,1,0:T(8,128)S(1)} fusion(f32[8,512]{1,0:T(8,128)S(1)} %get-tuple-element.308, f32[8,512]{1,0:T(8,128)S(1)} %get-tuple-element.305, pred[512,512]{1,0:T(8,128)(4,1)S(1)} %iota_compare_fusion.1, f32[8,128,512]{2,1,0:T(8,128)} %copy-done.3, f32[8,512]{1,0:T(8,128)S(1)} %get-tuple-element.259, f32[8,128]{1,0:T(8,128)S(1)} %get-tuple-element.306), kind=kOutput, calls=%fused_computation.19 | convolution fusion | flops 3232759808 | bytes 4509696 | tf_op jit(solution)/shard_map/lij,lxj->lxi/dot_general | solution.py:74
  79.3 1.3 copy-done.4
  81.0 4.3 %all-gather.4 = f32[16,128,1]{1,2,0:T(1,128)S(1)} all-gather(f32[8,128,1]{1,2,0:T(1,128)S(1)} %copy.27), channel_id=6, replica_groups=mesh['grp'=2,'gx'=4,'gy'=2,'hour'=2] {'gy'}, dimensions={0}, use_global_device_ids=true | all-gather | bytes 12288 | tf_op jit(solution)/shard_map/all_gather | solution.py:13
  87.1 4.9 %all-reduce.1 = f32[16]{0:T(128)S(1)} all-reduce(f32[16]{0:T(128)S(1)} %dynamic-update-slice.1), channel_id=5, replica_groups=mesh['grp'=2,'gx'=4,'gy'=2,'hour'=2] {'gy'}, use_global_device_ids=true, to_apply=%add.1 | all-reduce | flops 16 | bytes 128
  92.2 12.1 %fusion = f32[8,128,512]{2,1,0:T(8,128)S(1)} fusion(f32[8,512]{1,0:T(8,128)S(1)} %get-tuple-element.309, f32[8,512]{1,0:T(8,128)S(1)} %get-tuple-element.303, pred[512,512]{1,0:T(8,128)(4,1)S(1)} %iota_compare_fusion, f32[8,128,512]{2,1,0:T(8,128)} %copy-done.4, f32[8,512]{1,0:T(8,128)S(1)} %get-tuple-element.304, f32[8,128]{1,0:T(8,128)S(1)} %get-tuple-element.260), kind=kOutput, calls=%fused_computation.12 | convolution fusion | flops 3232759808 | bytes 4509696 | tf_op jit(solution)/shard_map/lij,lxj->lxi/dot_general | solution.py:79
  105.9 4.3 %all-gather.5 = f32[16,128,1]{1,2,0:T(1,128)S(1)} all-gather(f32[8,128,1]{1,2,0:T(1,128)S(1)} %copy.28), channel_id=7, replica_groups=mesh['grp'=2,'gx'=4,'gy'=2,'hour'=2] {'gy'}, dimensions={0}, use_global_device_ids=true | all-gather | bytes 12288 | tf_op jit(solution)/shard_map/all_gather | solution.py:13
  110.3 3.6 %convert_multiply_fusion = f32[8,128,512]{2,1,0:T(8,128)} fusion(bf16[8,128,512]{2,1,0:T(8,128)(2,1)} %param.18, f32[8,128,512]{2,1,0:T(8,128)} %copy-done.2, f32[8,512]{1,0:T(8,128)S(1)} %get-tuple-element.302, f32[8,128]{1,0:T(8,128)S(1)} %get-tuple-element.261), kind=kLoop, calls=%fused_computation.36 | loop fusion | flops 2097152 | bytes 5263360 | tf_op jit(solution)/shard_map/mul | solution.py:145
  113.9 17.9 %copy.37 = f32[8,128,512]{0,2,1:T(8,128)} copy(f32[8,128,512]{2,1,0:T(8,128)} %convert_multiply_fusion) | data formatting | bytes 4194304 | tf_op jit(solution)/shard_map/reshape | solution.py:103
  131.7 2.2 %scatter_custom_fusion = f32[512,128]{1,0:T(8,128)} fusion(s32[256]{0:T(256)S(1)} %compare_select_fusion.2, f32[256,128]{1,0:T(8,128)} %param.23, f32[]{:T(128)} %constant.140.clone.1), kind=kCustom, calls=%fused_computation.85 | custom fusion | bytes 262656 | tf_op jit(solution)/shard_map/scatter | solution.py:100
  133.9 3.4 %all-to-all-start = ((f32[8,64,128]{2,1,0:T(8,128)}), f32[8,64,128]{2,1,0:T(8,128)S(1)}, u32[]{:S(2)}, u32[]{:S(2)}) async-start(f32[8,64,128]{2,1,0:T(8,128)} %bitcast.14), calls=%async_computation | async-start | bytes 524288 | tf_op jit(solution)/shard_map/all_to_all | solution.py:104
  139.0 38.2 %gather_fusion = f32[8192,8]{1,0:T(8,128)} fusion(f32[8,65536]{0,1:T(8,128)} %bitcast.67, s32[8192]{0:T(1024)S(1)} %broadcast_clamp_fusion), kind=kCustom, calls=%fused_computation | custom fusion | bytes 557056 | tf_op jit(solution)/shard_map/jit(_take)/gather | solution.py:121
  177.3 2.8 %copy.36 = f32[8,512,16]{1,2,0:T(8,128)S(1)} copy(f32[8,512,16]{0,2,1:T(8,128)} %bitcast.68) | data formatting | bytes 524288 | tf_op jit(solution)/shard_map/jit(_take)/gather | solution.py:121
  181.5 5.9 %all-to-all-start.2 = ((f32[8,1,64]{2,1,0:T(1,128)}), f32[8,1,64]{2,1,0:T(1,128)S(1)}, u32[]{:S(2)}, u32[]{:S(2)}) async-start(f32[8,1,64]{2,1,0:T(1,128)} %all_to_all.14), calls=%async_computation.2 | async-start | bytes 8192 | tf_op jit(solution)/shard_map/all_to_all | solution.py:124
  187.4 6.5 %all-to-all-done.2 = f32[8,1,64]{2,1,0:T(1,128)S(1)} async-done(((f32[8,1,64]{2,1,0:T(1,128)}), f32[8,1,64]{2,1,0:T(1,128)S(1)}, u32[]{:S(2)}, u32[]{:S(2)}) %all-to-all-start.2) | async-done | bytes 2080 | tf_op jit(solution)/shard_map/all_to_all | solution.py:124
  195.1 1.9 gather_fusion.1
  197.1 2.5 %psum.7 = f32[256]{0:T(256)S(1)} all-reduce(f32[256]{0:T(256)S(1)} %and_select_fusion), channel_id=1, replica_groups=mesh['grp'=2,'gx'=4,'gy'=2,'hour'=2] {'hour'}, use_global_device_ids=true, to_apply=%region_15.16 | all-reduce | flops 256 | bytes 2048 | tf_op jit(solution)/shard_map/psum | solution.py:128
  (89 shorter events, 20.3 us)
Async XLA Ops:
  0.6 31.7 %copy-start = (f32[8,128,512]{2,1,0:T(8,128)S(1)}, f32[8,128,512]{2,1,0:T(8,128)}, u32[]{:S(2)}) copy-start(f32[8,128,512]{2,1,0:T(8,128)} %param.17) | copy-start | bytes 6291460
  5.2 128.7 %all-to-all-start.1 = ((s32[8,1,1024]{2,1,0:T(1,128)}), s32[8,1,1024]{2,1,0:T(1,128)S(1)}, u32[]{:S(2)}, u32[]{:S(2)}) async-start(s32[8,1,1024]{2,1,0:T(1,128)} %reshape.255), calls=%async_computation.1 | async-start | bytes 65536 | tf_op jit(solution)/shard_map/all_to_all | solution.py:111
  34.3 1.3 copy-start.1
  52.5 1.3 copy-start.3
  67.3 18.3 %copy-start.7 = (u32[32]{0:T(128)S(1)}, u32[32]{0:T(128)}, u32[]{:S(2)}) copy-start(u32[32]{0:T(128)} %constant.162) | copy-start | bytes 388
  79.3 1.3 copy-start.4
  104.3 1.3 copy-start.2
  133.9 46.4 %all-to-all-start = ((f32[8,64,128]{2,1,0:T(8,128)}), f32[8,64,128]{2,1,0:T(8,128)S(1)}, u32[]{:S(2)}, u32[]{:S(2)}) async-start(f32[8,64,128]{2,1,0:T(8,128)} %bitcast.14), calls=%async_computation | async-start | bytes 524288 | tf_op jit(solution)/shard_map/all_to_all | solution.py:104
  180.1 19.5 %copy-start.5 = (f32[256]{0:T(256)S(1)}, f32[256]{0:T(256)}, u32[]{:S(2)}) copy-start(f32[256]{0:T(256)} %param.25) | copy-start | bytes 3076
  180.1 19.4 %copy-start.6 = (f32[256]{0:T(256)S(1)}, f32[256]{0:T(256)}, u32[]{:S(2)}) copy-start(f32[256]{0:T(256)} %param.24) | copy-start | bytes 3076
  181.5 12.4 %all-to-all-start.2 = ((f32[8,1,64]{2,1,0:T(1,128)}), f32[8,1,64]{2,1,0:T(1,128)S(1)}, u32[]{:S(2)}, u32[]{:S(2)}) async-start(f32[8,1,64]{2,1,0:T(1,128)} %all_to_all.14), calls=%async_computation.2 | async-start | bytes 8192 | tf_op jit(solution)/shard_map/all_to_all | solution.py:124
where the time goes:
time: 201 us; the launch traced here: 200 us
  local copies, waits for them, and re-layouts  78.7 us (39%)
  blocking collectives  54.5 us (27%)
  matrix products  29.8 us (15%)
  starting transfers between devices  16.6 us (8%)
  other arithmetic  11.7 us (6%)
  waiting for transfers between devices  6.46 us (3%)
  between operations  2.25 us (1%)
    gather x2, local copies, waits for them, and re-layouts, observe(): jnp.take(flattened, cells_in.reshape(-1), axis=1)  41.1 us
    all_gather x4, blocking collectives, prefix(): gathered = jax.tree.map(lambda a: lax.all_gather(a, axis), part)  34.9 us
    reshape x1, local copies, waits for them, and re-layouts, observe(): flattened = increment.reshape(levels, -1)  17.9 us
    unnamed x2, blocking collectives  17.1 us
    dot_general x1, matrix products, filter_y(): inside = jnp.einsum('lij,lxj->lxi', matrix, smooth, precision=EXACT)  12.1 us
    dot_general x1, matrix products, filter_y(): inside = jnp.einsum('lij,lxj->lxi', matrix, along_x, precision=EXACT)  12 us
    unnamed x27, local copies, waits for them, and re-layouts  9.27 us
    all_to_all x1, starting transfers between devices, observe(): lax.all_to_all(send_cells.reshape(owners, capacity, points), ('gx', 'gy')...  7.25 us
  transfers between devices with their start and end apart: 3, of which 1 were waited for; matrix products, arithmetic and copies ran while one was open for 53% of the time, Pallas kernels for 0%

commit v1 on v0

v1 whole, which is shorter than its diff:
```python
import functools

import jax
import jax.numpy as jnp
from jax import lax
from jax.experimental import pallas as pl
from jax.experimental.pallas import tpu as pltpu
from jax.sharding import PartitionSpec as P

EXACT = lax.Precision.HIGHEST
MESH = pl.DeviceIdType.MESH
LANES = 128


def coefficients(rate):
    a = jnp.exp(-rate)
    series = jnp.ones_like(rate)
    small = jnp.minimum(rate, 0.5)
    for n in range(9, 1, -1):
        series = 1.0 - series * small * (1.0 / n)
    c = jnp.where(rate < 0.5, small * series, 1.0 - a)
    b = jnp.sqrt(c * (1.0 + a))
    return a, b, c


def pick(row, index):
    return jnp.take_along_axis(row, index, axis=1, mode="promise_in_bounds")


def combine(edges, carries, count, width):
    zero = tuple(jnp.zeros(edges.shape[2:], jnp.float32) for _ in range(width))

    def ahead(e, state):
        for t in range(width):
            carries[e, t] = state[t]
        factor = edges[e, 2 * width]
        return tuple(factor * state[t] + edges[e, t] for t in range(width))

    def behind(k, state):
        e = count - 1 - k
        for t in range(width):
            carries[e, width + t] = state[t]
        factor = edges[e, 2 * width]
        cross = edges[e, 2 * width + 1]
        return tuple(
            factor * state[t] + (edges[e, width + t] + cross * carries[e, t])
            for t in range(width)
        )

    if count <= 8:
        state = zero
        for e in range(count):
            state = ahead(e, state)
        state = zero
        for k in range(count):
            state = behind(k, state)
    else:
        lax.fori_loop(0, count, ahead, zero)
        lax.fori_loop(0, count, behind, zero)


def kernel(
    dims,
    control,
    scale,
    rate_x_h,
    rate_y_h,
    owner_h,
    stencil_h,
    weights_h,
    innovation_h,
    sigma_h,
    out,
    departure,
    field,
    scale_v,
    zx,
    zy,
    v1x,
    v2x,
    v1y,
    v2y,
    edges_x,
    edges_y,
    carry_x,
    carry_y,
    send_obs,
    recv_obs,
    codes_v,
    codes_s,
    acc,
    send_ret,
    recv_ret,
    rate_x,
    rate_y,
    owner,
    stencil,
    weights,
    innovation,
    sigma,
    small_sem,
    in_sem,
    out_sem,
    scale_sem,
    code_sem,
    xs,
    xr,
    ys,
    yr,
    os_,
    or_,
    rs,
    rr,
):
    nx, ny, nh, cap = dims
    owners = nx * ny
    levels, cx, cy = control.shape
    tiles = cy // LANES
    obs = owner.shape[1]
    mx, my, mh = lax.axis_index("gx"), lax.axis_index("gy"), lax.axis_index("hour")
    me = mx * ny + my
    world = owners * nh
    rank = me * nh + mh

    barrier = pltpu.get_barrier_semaphore()

    def greet(j, _):
        other = lax.rem(rank + j, world)
        pl.semaphore_signal(
            barrier,
            inc=1,
            device_id={
                "gx": other // (ny * nh),
                "gy": lax.rem(other // nh, ny),
                "hour": lax.rem(other, nh),
            },
            device_id_type=MESH,
        )
        return 0

    def load(t, l):
        return pltpu.make_async_copy(
            control.at[l, :, pl.ds(t * LANES, LANES)],
            field.at[t, pl.ds(l * cx, cx), :],
            in_sem.at[t, l],
        )

    small = [
        pltpu.make_async_copy(source, place, small_sem.at[n])
        for n, (source, place) in enumerate(
            (
                (rate_x_h, rate_x),
                (owner_h, owner),
                (stencil_h, stencil),
                (weights_h, weights),
                (rate_y_h, rate_y),
                (innovation_h, innovation),
                (sigma_h, sigma),
            )
        )
    ]
    small[0].start()
    for t in range(tiles):
        for l in range(levels):
            load(t, l).start()
    for copy in small[1:]:
        copy.start()
    scale_copy = pltpu.make_async_copy(scale, scale_v, scale_sem)
    scale_copy.start()
    lax.fori_loop(1, world, greet, 0)

    lane = lax.broadcasted_iota(jnp.int32, (levels, LANES), 1)
    ones = jnp.ones((levels, LANES), jnp.float32)
    zeros = jnp.zeros((levels, LANES), jnp.float32)

    small[0].wait()
    ax, bx, cxg = coefficients(rate_x[...])
    for t in range(tiles):
        for l in range(levels):
            load(t, l).wait()

    def x_forward(i, state):
        at = lane * 0 + i
        a, b = pick(ax, at), pick(bx, at)
        row = pl.ds(pl.multiple_of(i * levels, levels), levels)
        new = []
        for t in range(tiles):
            s = a * state[t] + b * field[t, pl.ds(i, levels, stride=cx), :]
            zx[t, row, :] = s
            new.append(s)
        lead = a * state[tiles]
        v1x[row, :] = lead
        return tuple(new) + (lead,)

    state = lax.fori_loop(0, cx, x_forward, (zeros,) * tiles + (ones,), unroll=8)
    for t in range(tiles):
        edges_x[mx, t] = state[t]
    edges_x[mx, 2 * tiles] = state[tiles]

    def x_backward(k, state):
        i = cx - 1 - k
        at = lane * 0 + i
        a, c = pick(ax, at), pick(cxg, at)
        row = pl.ds(pl.multiple_of(i * levels, levels), levels)
        new = []
        for t in range(tiles):
            s = a * state[t] + c * zx[t, row, :]
            zx[t, row, :] = s
            new.append(s)
        cross = a * state[tiles] + c * v1x[row, :]
        v1x[row, :] = cross
        trail = a * state[tiles + 1]
        v2x[row, :] = trail
        return tuple(new) + (cross, trail)

    state = lax.fori_loop(0, cx, x_backward, (zeros,) * (tiles + 1) + (ones,), unroll=8)
    for t in range(tiles):
        edges_x[mx, tiles + t] = state[t]
    edges_x[mx, 2 * tiles + 1] = state[tiles]

    pl.semaphore_wait(barrier, world - 1)

    def x_copy(j, place):
        return pltpu.make_async_remote_copy(
            src_ref=edges_x.at[place],
            dst_ref=edges_x.at[place],
            send_sem=xs.at[j],
            recv_sem=xr.at[j],
            device_id={"gx": lax.rem(mx + j, nx)},
            device_id_type=MESH,
        )

    def x_start(j, _):
        x_copy(j, mx).start()
        return 0

    lax.fori_loop(1, nx, x_start, 0)

    for copy in small[1:]:
        copy.wait()
    own = owner[...]
    own_col = jnp.transpose(jnp.broadcast_to(own.astype(jnp.float32), (8, obs)))[:, :1]
    earlier = lax.broadcasted_iota(jnp.int32, (obs, obs), 0) < lax.broadcasted_iota(
        jnp.int32, (obs, obs), 1
    )
    same = earlier & (own_col == own.astype(jnp.float32))
    place = jnp.sum(jnp.where(same, 1.0, 0.0), axis=0, keepdims=True).astype(jnp.int32)
    cells = stencil[...]
    points = cells.shape[0]
    corner = jnp.min(cells, axis=0, keepdims=True)
    j_row = lax.broadcasted_iota(jnp.int32, (points, obs), 0)
    wanted = corner + (j_row // 4) * cy + lax.rem(j_row, 4)
    order = jnp.zeros((points, obs), jnp.int32)
    for s in range(1, points):
        order = jnp.where(cells[s : s + 1, :] == wanted, s, order)
    order = jnp.concatenate([order + points * l for l in range(levels)], axis=0)
    order = jnp.transpose(order.astype(jnp.float32)).astype(jnp.int32)
    sorted_weights = pick(weights[...], order)
    target = own * cap + place
    slots = owners * cap
    chosen = jnp.where(
        lax.broadcasted_iota(jnp.int32, (slots, obs), 0) == target, 1.0, 0.0
    )
    packed = jnp.dot(
        chosen, sorted_weights, precision=EXACT, preferred_element_type=jnp.float32
    )
    send_obs[:, :cap, :] = packed.reshape(owners, cap, LANES)
    of_owner = jnp.where(
        lax.broadcasted_iota(jnp.int32, (owners, obs), 0) == own, 1.0, 0.0
    )
    of_place = jnp.where(
        lax.broadcasted_iota(jnp.int32, (LANES, obs), 0) == place, 1.0, 0.0
    )
    codes = lax.dot_general(
        of_owner * corner.astype(jnp.float32),
        of_place,
        (((1,), (1,)), ((), ())),
        precision=EXACT,
        preferred_element_type=jnp.float32,
    )
    send_obs[:, cap:, :] = jnp.broadcast_to(codes[:, None, :], (owners, 8, LANES))
    recv_obs[me] = send_obs[me]

    def obs_copy(j, there, here):
        return pltpu.make_async_remote_copy(
            src_ref=send_obs.at[there],
            dst_ref=recv_obs.at[here],
            send_sem=os_.at[j],
            recv_sem=or_.at[j],
            device_id={"gx": there // ny, "gy": lax.rem(there, ny)},
            device_id_type=MESH,
        )

    def obs_start(j, _):
        obs_copy(j, lax.rem(me + j, owners), me).start()
        return 0

    lax.fori_loop(1, owners, obs_start, 0)

    def x_wait(j, _):
        x_copy(j, lax.rem(mx + nx - j, nx)).wait_recv()
        return 0

    lax.fori_loop(1, nx, x_wait, 0)
    combine(edges_x, carry_x, nx, tiles)
    front = [carry_x[mx, t] for t in range(tiles)]
    back = [carry_x[mx, tiles + t] for t in range(tiles)]

    def x_finish(i, _):
        row = pl.ds(pl.multiple_of(i * levels, levels), levels)
        lead, trail = v1x[row, :], v2x[row, :]
        for t in range(tiles):
            zx[t, row, :] = zx[t, row, :] + (lead * front[t] + trail * back[t])
        return 0

    lax.fori_loop(0, cx, x_finish, 0, unroll=8)

    for t in range(tiles):
        for l in range(levels):
            zy[t, pl.ds(l, LANES, stride=levels), :] = jnp.transpose(
                zx[t, pl.ds(l, cx, stride=levels), :]
            )

    gains = [
        coefficients(rate_y[:, pl.ds(pl.multiple_of(my * cy + t * LANES, LANES), LANES)])
        for t in range(tiles)
    ]

    def y_forward(j, state):
        at = lane * 0 + j
        row = pl.ds(pl.multiple_of(j * levels, levels), levels)
        new, leads = [], []
        for t in range(tiles):
            a, b = pick(gains[t][0], at), pick(gains[t][1], at)
            s = a * state[t] + b * zy[t, row, :]
            zy[t, row, :] = s
            new.append(s)
            lead = a * state[tiles + t]
            v1y[t, row, :] = lead
            leads.append(lead)
        return tuple(new + leads)

    state = lax.fori_loop(
        0, LANES, y_forward, (zeros,) * tiles + (ones,) * tiles, unroll=4
    )
    for t in range(tiles):
        edges_y[my * tiles + t, 0] = state[t]
        edges_y[my * tiles + t, 2] = state[tiles + t]

    def y_backward(k, state):
        j = LANES - 1 - k
        at = lane * 0 + j
        row = pl.ds(pl.multiple_of(j * levels, levels), levels)
        new, crosses, trails = [], [], []
        for t in range(tiles):
            a, c = pick(gains[t][0], at), pick(gains[t][2], at)
            s = a * state[t] + c * zy[t, row, :]
            zy[t, row, :] = s
            new.append(s)
            cross = a * state[tiles + t] + c * v1y[t, row, :]
            v1y[t, row, :] = cross
            crosses.append(cross)
            trail = a * state[2 * tiles + t]
            v2y[t, row, :] = trail
            trails.append(trail)
        return tuple(new + crosses + trails)

    state = lax.fori_loop(
        0, LANES, y_backward, (zeros,) * (2 * tiles) + (ones,) * tiles, unroll=4
    )
    for t in range(tiles):
        edges_y[my * tiles + t, 1] = state[t]
        edges_y[my * tiles + t, 3] = state[tiles + t]

    def y_copy(j, there):
        part = edges_y.at[pl.ds(there * tiles, tiles)]
        return pltpu.make_async_remote_copy(
            src_ref=part,
            dst_ref=part,
            send_sem=ys.at[j],
            recv_sem=yr.at[j],
            device_id={"gy": lax.rem(my + j, ny)},
            device_id_type=MESH,
        )

    for j in range(1, ny):
        y_copy(j, my).start()

    def obs_wait(j, _):
        obs_copy(j, lax.rem(me + j, owners), lax.rem(me + owners - j, owners)).wait_recv()
        return 0

    lax.fori_loop(1, owners, obs_wait, 0)
    codes_v[...] = recv_obs[:, cap, :].astype(jnp.int32)
    code_copy = pltpu.make_async_copy(codes_v, codes_s, code_sem)
    code_copy.start()
    send_ret[...] = jnp.zeros(send_ret.shape, jnp.float32)
    scale_copy.wait()

    for j in range(1, ny):
        y_copy(j, lax.rem(my + ny - j, ny)).wait_recv()
    combine(edges_y, carry_y, ny * tiles, 1)

    for t in range(tiles):
        front_y = carry_y[my * tiles + t, 0]
        back_y = carry_y[my * tiles + t, 1]

        def y_finish(j, _, t=t, front_y=front_y, back_y=back_y):
            row = pl.ds(pl.multiple_of(j * levels, levels), levels)
            zy[t, row, :] = zy[t, row, :] + (
                v1y[t, row, :] * front_y + v2y[t, row, :] * back_y
            )
            return 0

        lax.fori_loop(0, LANES, y_finish, 0, unroll=8)

    def store(t, l):
        return pltpu.make_async_copy(
            field.at[t, pl.ds(l * cx, cx), :],
            out.at[l, :, pl.ds(t * LANES, LANES)],
            out_sem.at[t, l],
        )

    for t in range(tiles):
        for l in range(levels):
            block = jnp.transpose(zy[t, pl.ds(l, LANES, stride=levels), :])
            field[t, pl.ds(l * cx, cx), :] = block * scale_v[
                l, :, pl.ds(t * LANES, LANES)
            ].astype(jnp.float32)
            store(t, l).start()

    code_copy.wait()
    level_base = lax.broadcasted_iota(jnp.int32, (levels, LANES), 0) * points
    shift = cy.bit_length() - 1

    def ret_copy(j, turn, there, here):
        return pltpu.make_async_remote_copy(
            src_ref=send_ret.at[there],
            dst_ref=recv_ret.at[turn, here],
            send_sem=rs.at[turn, j],
            recv_sem=rr.at[turn, j],
            device_id={
                "gx": there // ny,
                "gy": lax.rem(there, ny),
                "hour": lax.rem(mh + turn, nh),
            },
            device_id_type=MESH,
        )

    def one_source(source):
        def one_slot(p, _):
            code = codes_s[source, p]
            u = jnp.minimum((code >> shift) & (cx - 1), cx - 4)
            v = code & (cy - 1)
            tile = v >> 7
            off = v & (LANES - 1)
            after = jnp.minimum(tile + 1, tiles - 1)
            row = jnp.broadcast_to(recv_obs[source, pl.ds(p, 1), :], (levels, LANES))
            ahead = (lane - off) & (LANES - 1)
            base = level_base + (ahead & 3)
            inside = lane >= off
            total = None
            for dx in range(4):
                rows = pl.ds(u + dx, levels, stride=cx)
                data = jnp.where(inside, field[tile, rows, :], field[after, rows, :])
                term = pick(row, base + 4 * dx) * data
                total = term if total is None else total + term
            acc[pl.ds(pl.multiple_of(p * levels, levels), levels), :] = jnp.where(
                ahead < 4, total, 0.0
            )
            return 0

        lax.fori_loop(0, cap, one_slot, 0, unroll=8)
        summed = acc[pl.ds(0, cap, stride=levels), :]
        for l in range(1, levels):
            summed = summed + acc[pl.ds(l, cap, stride=levels), :]
        return lax.dot_general(
            ones,
            summed,
            (((1,), (1,)), ((), ())),
            precision=EXACT,
            preferred_element_type=jnp.float32,
        )

    def each_source(j, _):
        source = lax.rem(me + j, owners)
        send_ret[source, :, :cap] = one_source(source)
        for turn in range(nh):
            ret_copy(j, turn, source, me).start()
        return 0

    lax.fori_loop(1, owners, each_source, 0)
    send_ret[me, :, :cap] = one_source(me)
    for turn in range(1, nh):
        ret_copy(0, turn, me, me).start()
    recv_ret[0, me] = send_ret[me]

    for turn in range(1, nh):
        ret_copy(0, turn, me, me).wait_recv()

    def ret_wait(j, _):
        for turn in range(nh):
            ret_copy(
                j, turn, lax.rem(me + j, owners), lax.rem(me + owners - j, owners)
            ).wait_recv()
        return 0

    lax.fori_loop(1, owners, ret_wait, 0)
    back_sum = recv_ret[0, :, 0, :cap]
    for turn in range(1, nh):
        back_sum = back_sum + recv_ret[turn, :, 0, :cap]
    spread = jnp.dot(
        back_sum, of_place[:cap], precision=EXACT, preferred_element_type=jnp.float32
    )
    modelled = jnp.sum(spread * of_owner, axis=0, keepdims=True)
    departure[...] = (modelled - innovation[...]) / sigma[...]

    for t in range(tiles):
        for l in range(levels):
            store(t, l).wait()

    def x_sent(j, _):
        x_copy(j, mx).wait_send()
        return 0

    lax.fori_loop(1, nx, x_sent, 0)
    for j in range(1, ny):
        y_copy(j, my).wait_send()

    def obs_sent(j, _):
        obs_copy(j, lax.rem(me + j, owners), me).wait_send()
        for turn in range(nh):
            ret_copy(j, turn, lax.rem(me + j, owners), me).wait_send()
        return 0

    lax.fori_loop(1, owners, obs_sent, 0)
    for turn in range(1, nh):
        ret_copy(0, turn, me, me).wait_send()


def on_device(
    dims, control, background_scale, rate_x, rate_y, obs_owner, stencil, obs_weights, innovation, obs_sigma
):
    nx, ny, nh = dims
    owners = nx * ny
    levels, cx, cy = control.shape
    tiles = cy // LANES
    obs = obs_owner.shape[0]
    cap = -(-(2 * obs // owners) // 8) * 8
    f32 = jnp.float32
    vmem = pl.BlockSpec(memory_space=pltpu.VMEM)
    hbm = pl.BlockSpec(memory_space=pl.ANY)
    dma = pltpu.SemaphoreType.DMA
    increment, departure = pl.pallas_call(
        functools.partial(kernel, (nx, ny, nh, cap)),
        out_shape=(
            jax.ShapeDtypeStruct(control.shape, f32),
            jax.ShapeDtypeStruct((1, obs), f32),
        ),
        in_specs=[hbm] * 9,
        out_specs=(hbm, vmem),
        scratch_shapes=[
            pltpu.VMEM((tiles, levels * cx, LANES), f32),
            pltpu.VMEM((levels, cx, cy), background_scale.dtype),
            pltpu.VMEM((tiles, cx * levels, LANES), f32),
            pltpu.VMEM((tiles, LANES * levels, cx), f32),
            pltpu.VMEM((cx * levels, LANES), f32),
            pltpu.VMEM((cx * levels, LANES), f32),
            pltpu.VMEM((tiles, LANES * levels, cx), f32),
            pltpu.VMEM((tiles, LANES * levels, cx), f32),
            pltpu.VMEM((nx, 2 * tiles + 2, levels, LANES), f32),
            pltpu.VMEM((ny * tiles, 4, levels, cx), f32),
            pltpu.VMEM((nx, 2 * tiles, levels, LANES), f32),
            pltpu.VMEM((ny * tiles, 2, levels, cx), f32),
            pltpu.VMEM((owners, cap + 8, LANES), f32),
            pltpu.VMEM((owners, cap + 8, LANES), f32),
            pltpu.VMEM((owners, LANES), jnp.int32),
            pltpu.SMEM((owners, LANES), jnp.int32),
            pltpu.VMEM((cap * levels, LANES), f32),
            pltpu.VMEM((owners, 8, LANES), f32),
            pltpu.VMEM((nh, owners, 8, LANES), f32),
            pltpu.VMEM(rate_x.shape, f32),
            pltpu.VMEM(rate_y.shape, f32),
            pltpu.VMEM((1, obs), jnp.int32),
            pltpu.VMEM((stencil.shape[1], obs), jnp.int32),
            pltpu.VMEM(obs_weights.shape, f32),
            pltpu.VMEM((1, obs), f32),
            pltpu.VMEM((1, obs), f32),
            dma((7,)),
            dma((tiles, levels)),
            dma((tiles, levels)),
            dma,
            dma,
            dma((nx,)),
            dma((nx,)),
            dma((ny,)),
            dma((ny,)),
            dma((owners,)),
            dma((owners,)),
            dma((nh, owners)),
            dma((nh, owners)),
        ],
        compiler_params=pltpu.CompilerParams(
            collective_id=0, has_side_effects=True, vmem_limit_bytes=56 * 1024 * 1024
        ),
    )(
        control,
        background_scale,
        rate_x,
        rate_y,
        obs_owner.reshape(1, obs),
        stencil.T,
        obs_weights,
        innovation.reshape(1, obs),
        obs_sigma.reshape(1, obs),
    )
    return increment, departure.reshape(obs)


def solution(mesh):
    dims = (mesh.shape["gx"], mesh.shape["gy"], mesh.shape["hour"])
    return jax.shard_map(
        functools.partial(on_device, dims),
        mesh=mesh,
        in_specs=(
            P(("grp", "hour"), "gx", "gy"),
            P(("grp", "hour"), "gx", "gy"),
            P(("grp", "hour"), "gx"),
            P(("grp", "hour"), None),
            P(("grp", "gx", "gy")),
            P(("grp", "gx", "gy"), None),
            P(("grp", "gx", "gy"), "hour"),
            P(("grp", "gx", "gy")),
            P(("grp", "gx", "gy")),
        ),
        out_specs=(P(("grp", "hour"), "gx", "gy"), P(("grp", "gx", "gy"))),
        check_vma=False,
    )
```

time: 201 us -> 50.4 us (0.25)
  local copies, waits for them, and re-layouts: 78.7 us -> 3.65 us
  blocking collectives: 54.5 us -> 0 us
  Pallas kernels: 0 us -> 45.3 us
  matrix products: 29.8 us -> 0 us
  starting transfers between devices: 16.6 us -> 0 us
  other arithmetic: 11.7 us -> 0 us
  waiting for transfers between devices: 6.46 us -> 0 us
    pallas_call x0 -> x1, Pallas kernels: none -> 45.3 us  [on_device(): pl.pallas_call(functools.partial(kernel, (nx, ny, nh, cap)), out_shape=(j...]
    gather x3 -> x0, local copies, waits for them, and re-layouts: 43 us -> none  [the longest x2 41.1 us: observe(): jnp.take(flattened, cells_in.reshape(-1), axis=1)]
    all_gather x4 -> x0, blocking collectives: 34.9 us -> none  [prefix(): gathered = jax.tree.map(lambda a: lax.all_gather(a, axis), part)]
    dot_general x4 -> x0, matrix products: 29.8 us -> none  [the longest x1 12.1 us: filter_y(): inside = jnp.einsum('lij,lxj->lxi', matrix, smooth, precision=EXACT)]
    reshape x6 -> x0, local copies, waits for them, and re-layouts: 19.1 us -> none  [the longest x1 17.9 us: observe(): flattened = increment.reshape(levels, -1)]
    unnamed x2 -> x0, blocking collectives: 17.1 us -> none
    all_to_all x3 -> x0, starting transfers between devices: 16.6 us -> none  [the longest x1 7.25 us: observe(): lax.all_to_all(send_cells.reshape(owners, capacity, points), ('gx', 'gy')...]
    all_to_all x3 -> x0, waiting for transfers between devices: 6.46 us -> none  [the longest x1 6.46 us: observe(): lax.all_to_all(summed.reshape(sources, item_count), ('gx', 'gy'), split_a...]
  transfers between devices with their start and end apart: 3 -> 0, of which waited for: 1 -> 0; matrix products, arithmetic and copies ran while one was open for 53% -> 0% of each run, Pallas kernels for 0% -> 0%
where the time goes in v1:
time: 50.4 us; the launch traced here: 49.6 us
  Pallas kernels  45.3 us (90%)
  local copies, waits for them, and re-layouts  3.65 us (7%)
  between operations  0.65 us (1%)
    pallas_call x1, Pallas kernels, on_device(): pl.pallas_call(functools.partial(kernel, (nx, ny, nh, cap)), out_shape=(j...  45.3 us
    unnamed x4, local copies, waits for them, and re-layouts  3.65 us

profile of v1, /device:TPU:0, one launch (start us, length us, event | category | flops | bytes accessed | tf_op | source)
XLA Modules:
  0.0 49.6 jit_solution(14420193696677133932)
XLA Ops:
  0.6 45.3 %shard_map.104 = (f32[8,128,512]{2,1,0:T(8,128)}, f32[1,256]{1,0:T(1,128)}) custom-call(f32[8,128,512]{2,1,0:T(8,128)} %control.1, bf16[8,128,512]{2,1,0:T(8,128)(2,1)} %scale.1, f32[8,128]{1,0:T(8,128)} %rate_x_h.1, f32[8,1024]{1,0:T(8,128)} %rate_y_h.1, s32[1,256]{1,0:T(1,128)} %bitcast.6, s32[16,256]{1,0:T(8,128)} %bitcast.5, f32[256,128]{1,0:T(8,128)} %weights_h.1, ...), custom_call_target="tpu_custom_call" | custom-call | tf_op jit(solution)/shard_map/pallas_call | solution.py:554
  46.0 0.0 copy-start
  46.0 3.1 %copy.13 = f32[8,128,512]{2,1,0:T(8,128)} copy(f32[8,128,512]{2,1,0:T(8,128)} %get-tuple-element.8) | data formatting | bytes 4194304
  49.1 0.0 copy-done
  49.1 0.6 %copy.14 = f32[256]{0:T(256)} copy(f32[256]{0:T(256)S(1)} %bitcast.9) | data formatting | bytes 2048
Async XLA Ops:
  46.0 3.1 %copy-start = (f32[1,256]{1,0:T(1,128)S(1)}, f32[1,256]{1,0:T(1,128)}, u32[]{:S(2)}) copy-start(f32[1,256]{1,0:T(1,128)} %get-tuple-element.5) | copy-start | bytes 3076

commit v2 on v1

--- a/solution.py
+++ b/solution.py
@@ -27,36 +27,30 @@
     return jnp.take_along_axis(row, index, axis=1, mode="promise_in_bounds")
 
 
-def combine(edges, carries, count, width):
-    zero = tuple(jnp.zeros(edges.shape[2:], jnp.float32) for _ in range(width))
+def combine(arrived, carries, count, needed, width):
+    zero = tuple(jnp.zeros(carries.shape[2:], jnp.float32) for _ in range(width))
 
     def ahead(e, state):
+        factor = arrived(e, 0, width)
+        new = []
         for t in range(width):
             carries[e, t] = state[t]
-        factor = edges[e, 2 * width]
-        return tuple(factor * state[t] + edges[e, t] for t in range(width))
+            new.append(factor * state[t] + arrived(e, 0, t))
+        return tuple(new)
 
     def behind(k, state):
         e = count - 1 - k
+        factor, cross = arrived(e, 0, width), arrived(e, 1, width)
+        new = []
         for t in range(width):
             carries[e, width + t] = state[t]
-        factor = edges[e, 2 * width]
-        cross = edges[e, 2 * width + 1]
-        return tuple(
-            factor * state[t] + (edges[e, width + t] + cross * carries[e, t])
-            for t in range(width)
-        )
-
-    if count <= 8:
-        state = zero
-        for e in range(count):
-            state = ahead(e, state)
-        state = zero
-        for k in range(count):
-            state = behind(k, state)
-    else:
-        lax.fori_loop(0, count, ahead, zero)
-        lax.fori_loop(0, count, behind, zero)
+            new.append(
+                factor * state[t] + (arrived(e, 1, t) + cross * carries[e, t])
+            )
+        return tuple(new)
+
+    lax.fori_loop(0, count, ahead, zero)
+    lax.fori_loop(0, needed, behind, zero)
 
 
 def kernel(
@@ -80,6 +74,9 @@
     v2x,
     v1y,
     v2y,
+    ay,
+    by,
+    cyg,
     edges_x,
     edges_y,
     carry_x,
@@ -89,6 +86,7 @@
     codes_v,
     codes_s,
     acc,
+    sums,
     send_ret,
     recv_ret,
     rate_x,
@@ -194,8 +192,25 @@
 
     state = lax.fori_loop(0, cx, x_forward, (zeros,) * tiles + (ones,), unroll=8)
     for t in range(tiles):
-        edges_x[mx, t] = state[t]
-    edges_x[mx, 2 * tiles] = state[tiles]
+        edges_x[mx, 0, t] = state[t]
+    edges_x[mx, 0, tiles] = state[tiles]
+    pl.semaphore_wait(barrier, world - 1)
+
+    def x_copy(half, j, place, there):
+        return pltpu.make_async_remote_copy(
+            src_ref=edges_x.at[place, half],
+            dst_ref=edges_x.at[place, half],
+            send_sem=xs.at[half, j],
+            recv_sem=xr.at[half, j],
+            device_id={"gx": there},
+            device_id_type=MESH,
+        )
+
+    def x_start(j, _):
+        x_copy(0, j, mx, lax.rem(mx + j, nx)).start()
+        return 0
+
+    lax.fori_loop(1, nx, x_start, 0)
 
     def x_backward(k, state):
         i = cx - 1 - k
@@ -215,26 +230,14 @@
 
     state = lax.fori_loop(0, cx, x_backward, (zeros,) * (tiles + 1) + (ones,), unroll=8)
     for t in range(tiles):
-        edges_x[mx, tiles + t] = state[t]
-    edges_x[mx, 2 * tiles + 1] = state[tiles]
-
-    pl.semaphore_wait(barrier, world - 1)
-
-    def x_copy(j, place):
-        return pltpu.make_async_remote_copy(
-            src_ref=edges_x.at[place],
-            dst_ref=edges_x.at[place],
-            send_sem=xs.at[j],
-            recv_sem=xr.at[j],
-            device_id={"gx": lax.rem(mx + j, nx)},
-            device_id_type=MESH,
-        )
-
-    def x_start(j, _):
-        x_copy(j, mx).start()
-        return 0
-
-    lax.fori_loop(1, nx, x_start, 0)
+        edges_x[mx, 1, t] = state[t]
+    edges_x[mx, 1, tiles] = state[tiles]
+
+    def x_start_back(j, _):
+        x_copy(1, j, mx, mx - j).start()
+        return 0
+
+    lax.fori_loop(1, mx + 1, x_start_back, 0)
 
     for copy in small[1:]:
         copy.wait()
@@ -297,12 +300,51 @@
 
     lax.fori_loop(1, owners, obs_start, 0)
 
+    for t in range(tiles):
+        gains = coefficients(
+            rate_y[:, pl.ds(pl.multiple_of(my * cy + t * LANES, LANES), LANES)]
+        )
+
+        def y_lead(j, lead, t=t, gains=gains):
+            at = lane * 0 + j
+            row = pl.ds(pl.multiple_of(j * levels, levels), levels)
+            a = pick(gains[0], at)
+            ay[t, row, :] = a
+            by[t, row, :] = pick(gains[1], at)
+            lead = a * lead
+            v1y[t, row, :] = lead
+            return lead
+
+        edges_y[my, 0, tiles + t] = lax.fori_loop(0, LANES, y_lead, ones, unroll=8)
+
+        def y_cross(k, state, t=t, gains=gains):
+            j = LANES - 1 - k
+            at = lane * 0 + j
+            row = pl.ds(pl.multiple_of(j * levels, levels), levels)
+            a, c = ay[t, row, :], pick(gains[2], at)
+            cyg[t, row, :] = c
+            cross = a * state[0] + c * v1y[t, row, :]
+            v1y[t, row, :] = cross
+            trail = a * state[1]
+            v2y[t, row, :] = trail
+            return cross, trail
+
+        edges_y[my, 1, tiles + t] = lax.fori_loop(
+            0, LANES, y_cross, (zeros, ones), unroll=8
+        )[0]
+
     def x_wait(j, _):
-        x_copy(j, lax.rem(mx + nx - j, nx)).wait_recv()
+        x_copy(0, j, lax.rem(mx + nx - j, nx), lax.rem(mx + j, nx)).wait_recv()
         return 0
 
     lax.fori_loop(1, nx, x_wait, 0)
-    combine(edges_x, carry_x, nx, tiles)
+
+    def x_wait_back(j, _):
+        x_copy(1, j, mx + j, lax.rem(mx + j, nx)).wait_recv()
+        return 0
+
+    lax.fori_loop(1, nx - mx, x_wait_back, 0)
+    combine(lambda e, half, t: edges_x[e, half, t], carry_x, nx, nx - mx, tiles)
     front = [carry_x[mx, t] for t in range(tiles)]
     back = [carry_x[mx, tiles + t] for t in range(tiles)]
 
@@ -321,70 +363,51 @@
                 zx[t, pl.ds(l, cx, stride=levels), :]
             )
 
-    gains = [
-        coefficients(rate_y[:, pl.ds(pl.multiple_of(my * cy + t * LANES, LANES), LANES)])
-        for t in range(tiles)
-    ]
-
     def y_forward(j, state):
-        at = lane * 0 + j
         row = pl.ds(pl.multiple_of(j * levels, levels), levels)
-        new, leads = [], []
+        new = []
         for t in range(tiles):
-            a, b = pick(gains[t][0], at), pick(gains[t][1], at)
-            s = a * state[t] + b * zy[t, row, :]
-            zy[t, row, :] = s
-            new.append(s)
-            lead = a * state[tiles + t]
-            v1y[t, row, :] = lead
-            leads.append(lead)
-        return tuple(new + leads)
-
-    state = lax.fori_loop(
-        0, LANES, y_forward, (zeros,) * tiles + (ones,) * tiles, unroll=4
-    )
-    for t in range(tiles):
-        edges_y[my * tiles + t, 0] = state[t]
-        edges_y[my * tiles + t, 2] = state[tiles + t]
+            value = ay[t, row, :] * state[t] + by[t, row, :] * zy[t, row, :]
+            zy[t, row, :] = value
+            new.append(value)
+        return tuple(new)
+
+    state = lax.fori_loop(0, LANES, y_forward, (zeros,) * tiles, unroll=8)
+    for t in range(tiles):
+        edges_y[my, 0, t] = state[t]
+
+    def y_copy(half, j, place, there):
+        return pltpu.make_async_remote_copy(
+            src_ref=edges_y.at[place, half],
+            dst_ref=edges_y.at[place, half],
+            send_sem=ys.at[half, j],
+            recv_sem=yr.at[half, j],
+            device_id={"gy": there},
+            device_id_type=MESH,
+        )
+
+    for j in range(1, ny):
+        y_copy(0, j, my, lax.rem(my + j, ny)).start()
 
     def y_backward(k, state):
         j = LANES - 1 - k
-        at = lane * 0 + j
         row = pl.ds(pl.multiple_of(j * levels, levels), levels)
-        new, crosses, trails = [], [], []
+        new = []
         for t in range(tiles):
-            a, c = pick(gains[t][0], at), pick(gains[t][2], at)
-            s = a * state[t] + c * zy[t, row, :]
-            zy[t, row, :] = s
-            new.append(s)
-            cross = a * state[tiles + t] + c * v1y[t, row, :]
-            v1y[t, row, :] = cross
-            crosses.append(cross)
-            trail = a * state[2 * tiles + t]
-            v2y[t, row, :] = trail
-            trails.append(trail)
-        return tuple(new + crosses + trails)
-
-    state = lax.fori_loop(
-        0, LANES, y_backward, (zeros,) * (2 * tiles) + (ones,) * tiles, unroll=4
-    )
-    for t in range(tiles):
-        edges_y[my * tiles + t, 1] = state[t]
-        edges_y[my * tiles + t, 3] = state[tiles + t]
-
-    def y_copy(j, there):
-        part = edges_y.at[pl.ds(there * tiles, tiles)]
-        return pltpu.make_async_remote_copy(
-            src_ref=part,
-            dst_ref=part,
-            send_sem=ys.at[j],
-            recv_sem=yr.at[j],
-            device_id={"gy": lax.rem(my + j, ny)},
-            device_id_type=MESH,
-        )
-
-    for j in range(1, ny):
-        y_copy(j, my).start()
+            value = ay[t, row, :] * state[t] + cyg[t, row, :] * zy[t, row, :]
+            zy[t, row, :] = value
+            new.append(value)
+        return tuple(new)
+
+    state = lax.fori_loop(0, LANES, y_backward, (zeros,) * tiles, unroll=8)
+    for t in range(tiles):
+        edges_y[my, 1, t] = state[t]
+
+    def y_start_back(j, _):
+        y_copy(1, j, my, my - j).start()
+        return 0
+
+    lax.fori_loop(1, my + 1, y_start_back, 0)
 
     def obs_wait(j, _):
         obs_copy(j, lax.rem(me + j, owners), lax.rem(me + owners - j, owners)).wait_recv()
@@ -394,12 +417,23 @@
     codes_v[...] = recv_obs[:, cap, :].astype(jnp.int32)
     code_copy = pltpu.make_async_copy(codes_v, codes_s, code_sem)
     code_copy.start()
-    send_ret[...] = jnp.zeros(send_ret.shape, jnp.float32)
     scale_copy.wait()
 
     for j in range(1, ny):
-        y_copy(j, lax.rem(my + ny - j, ny)).wait_recv()
-    combine(edges_y, carry_y, ny * tiles, 1)
+        y_copy(0, j, lax.rem(my + ny - j, ny), lax.rem(my + j, ny)).wait_recv()
+
+    def y_wait_back(j, _):
+        y_copy(1, j, my + j, lax.rem(my + j, ny)).wait_recv()
+        return 0
+
+    lax.fori_loop(1, ny - my, y_wait_back, 0)
+    combine(
+        lambda e, half, t: edges_y[e // tiles, half, t * tiles + lax.rem(e, tiles)],
+        carry_y,
+        ny * tiles,
+        (ny - my) * tiles,
+        1,
+    )
 
     for t in range(tiles):
         front_y = carry_y[my * tiles + t, 0]
@@ -424,9 +458,9 @@
     for t in range(tiles):
         for l in range(levels):
             block = jnp.transpose(zy[t, pl.ds(l, LANES, stride=levels), :])
-            field[t, pl.ds(l * cx, cx), :] = block * scale_v[
-                l, :, pl.ds(t * LANES, LANES)
-            ].astype(jnp.float32)
+            block = block * scale_v[l, :, pl.ds(t * LANES, LANES)].astype(jnp.float32)
+            field[t, pl.ds(l * cx, cx), :] = block
+            zx[t, pl.ds(l, cx, stride=levels), :] = block
             store(t, l).start()
 
     code_copy.wait()
@@ -435,7 +469,7 @@
 
     def ret_copy(j, turn, there, here):
         return pltpu.make_async_remote_copy(
-            src_ref=send_ret.at[there],
+            src_ref=send_ret.at[there * cap // LANES],
             dst_ref=recv_ret.at[turn, here],
             send_sem=rs.at[turn, j],
             recv_sem=rr.at[turn, j],
@@ -461,8 +495,8 @@
             inside = lane >= off
             total = None
             for dx in range(4):
-                rows = pl.ds(u + dx, levels, stride=cx)
-                data = jnp.where(inside, field[tile, rows, :], field[after, rows, :])
+                rows = pl.ds((u + dx) * levels, levels)
+                data = jnp.where(inside, zx[tile, rows, :], zx[after, rows, :])
                 term = pick(row, base + 4 * dx) * data
                 total = term if total is None else total + term
             acc[pl.ds(pl.multiple_of(p * levels, levels), levels), :] = jnp.where(
@@ -474,26 +508,31 @@
         summed = acc[pl.ds(0, cap, stride=levels), :]
         for l in range(1, levels):
             summed = summed + acc[pl.ds(l, cap, stride=levels), :]
-        return lax.dot_general(
+        sums[pl.ds(pl.multiple_of(source * cap, 8), cap), :] = summed
+
+    def each_source(source, _):
+        one_source(source)
+        return 0
+
+    lax.fori_loop(0, owners, each_source, 0)
+    for n in range(slots // LANES):
+        send_ret[n] = lax.dot_general(
             ones,
-            summed,
+            sums[n * LANES : (n + 1) * LANES, :],
             (((1,), (1,)), ((), ())),
             precision=EXACT,
             preferred_element_type=jnp.float32,
         )
 
-    def each_source(j, _):
-        source = lax.rem(me + j, owners)
-        send_ret[source, :, :cap] = one_source(source)
+    def ret_start(j, _):
         for turn in range(nh):
-            ret_copy(j, turn, source, me).start()
-        return 0
-
-    lax.fori_loop(1, owners, each_source, 0)
-    send_ret[me, :, :cap] = one_source(me)
+            ret_copy(j, turn, lax.rem(me + j, owners), me).start()
+        return 0
+
+    lax.fori_loop(1, owners, ret_start, 0)
     for turn in range(1, nh):
         ret_copy(0, turn, me, me).start()
-    recv_ret[0, me] = send_ret[me]
+    recv_ret[0, me] = send_ret[me * cap // LANES]
 
     for turn in range(1, nh):
         ret_copy(0, turn, me, me).wait_recv()
@@ -506,11 +545,17 @@
         return 0
 
     lax.fori_loop(1, owners, ret_wait, 0)
-    back_sum = recv_ret[0, :, 0, :cap]
+    back_sum = recv_ret[0, :, 0, :]
     for turn in range(1, nh):
-        back_sum = back_sum + recv_ret[turn, :, 0, :cap]
+        back_sum = back_sum + recv_ret[turn, :, 0, :]
+    of_lane = jnp.where(
+        lax.broadcasted_iota(jnp.int32, (LANES, obs), 0)
+        == place + lax.rem(me * cap, LANES),
+        1.0,
+        0.0,
+    )
     spread = jnp.dot(
-        back_sum, of_place[:cap], precision=EXACT, preferred_element_type=jnp.float32
+        back_sum, of_lane, precision=EXACT, preferred_element_type=jnp.float32
     )
     modelled = jnp.sum(spread * of_owner, axis=0, keepdims=True)
     departure[...] = (modelled - innovation[...]) / sigma[...]
@@ -520,12 +565,24 @@
             store(t, l).wait()
 
     def x_sent(j, _):
-        x_copy(j, mx).wait_send()
+        x_copy(0, j, mx, lax.rem(mx + j, nx)).wait_send()
         return 0
 
     lax.fori_loop(1, nx, x_sent, 0)
+
+    def x_sent_back(j, _):
+        x_copy(1, j, mx, mx - j).wait_send()
+        return 0
+
+    lax.fori_loop(1, mx + 1, x_sent_back, 0)
     for j in range(1, ny):
-        y_copy(j, my).wait_send()
+        y_copy(0, j, my, lax.rem(my + j, ny)).wait_send()
+
+    def y_sent_back(j, _):
+        y_copy(1, j, my, my - j).wait_send()
+        return 0
+
+    lax.fori_loop(1, my + 1, y_sent_back, 0)
 
     def obs_sent(j, _):
         obs_copy(j, lax.rem(me + j, owners), me).wait_send()
@@ -549,7 +606,7 @@
     cap = -(-(2 * obs // owners) // 8) * 8
     f32 = jnp.float32
     vmem = pl.BlockSpec(memory_space=pltpu.VMEM)
-    hbm = pl.BlockSpec(memory_space=pl.ANY)
+    hbm = pl.BlockSpec(memory_space=pltpu.HBM)
     dma = pltpu.SemaphoreType.DMA
     increment, departure = pl.pallas_call(
         functools.partial(kernel, (nx, ny, nh, cap)),
@@ -558,7 +615,7 @@
             jax.ShapeDtypeStruct((1, obs), f32),
         ),
         in_specs=[hbm] * 9,
-        out_specs=(hbm, vmem),
+        out_specs=(pl.BlockSpec(memory_space=pl.ANY), vmem),
         scratch_shapes=[
             pltpu.VMEM((tiles, levels * cx, LANES), f32),
             pltpu.VMEM((levels, cx, cy), background_scale.dtype),
@@ -568,8 +625,11 @@
             pltpu.VMEM((cx * levels, LANES), f32),
             pltpu.VMEM((tiles, LANES * levels, cx), f32),
             pltpu.VMEM((tiles, LANES * levels, cx), f32),
-            pltpu.VMEM((nx, 2 * tiles + 2, levels, LANES), f32),
-            pltpu.VMEM((ny * tiles, 4, levels, cx), f32),
+            pltpu.VMEM((tiles, LANES * levels, LANES), f32),
+            pltpu.VMEM((tiles, LANES * levels, LANES), f32),
+            pltpu.VMEM((tiles, LANES * levels, LANES), f32),
+            pltpu.VMEM((nx, 2, tiles + 1, levels, LANES), f32),
+            pltpu.VMEM((ny, 2, 2 * tiles, levels, cx), f32),
             pltpu.VMEM((nx, 2 * tiles, levels, LANES), f32),
             pltpu.VMEM((ny * tiles, 2, levels, cx), f32),
             pltpu.VMEM((owners, cap + 8, LANES), f32),
@@ -577,7 +637,8 @@
             pltpu.VMEM((owners, LANES), jnp.int32),
             pltpu.SMEM((owners, LANES), jnp.int32),
             pltpu.VMEM((cap * levels, LANES), f32),
-            pltpu.VMEM((owners, 8, LANES), f32),
+            pltpu.VMEM((owners * cap, LANES), f32),
+            pltpu.VMEM((owners * cap // LANES, 8, LANES), f32),
             pltpu.VMEM((nh, owners, 8, LANES), f32),
             pltpu.VMEM(rate_x.shape, f32),
             pltpu.VMEM(rate_y.shape, f32),
@@ -591,10 +652,10 @@
             dma((tiles, levels)),
             dma,
             dma,
-            dma((nx,)),
-            dma((nx,)),
-            dma((ny,)),
-            dma((ny,)),
+            dma((2, nx)),
+            dma((2, nx)),
+            dma((2, ny)),
+            dma((2, ny)),
             dma((owners,)),
             dma((owners,)),
             dma((nh, owners)),

time: 50.4 us -> 53.1 us (1.054); the launches traced: 49.6 us -> 53 us
  Pallas kernels: 45.3 us -> 48.7 us
    pallas_call x1, Pallas kernels: 45.3 us -> 48.7 us  [on_device(): pl.pallas_call(functools.partial(kernel, (nx, ny, nh, cap)), out_shape=(j...]
where the time goes in v2:
time: 53.1 us; the launch traced here: 53 us
  Pallas kernels  48.7 us (92%)
  local copies, waits for them, and re-layouts  3.65 us (7%)
  between operations  0.65 us (1%)
    pallas_call x1, Pallas kernels, on_device(): pl.pallas_call(functools.partial(kernel, (nx, ny, nh, cap)), out_shape=(j...  48.7 us
    unnamed x4, local copies, waits for them, and re-layouts  3.65 us

profile of v2, /device:TPU:0, one launch (start us, length us, event | category | flops | bytes accessed | tf_op | source)
XLA Modules:
  0.0 53.0 jit_solution(11379179898775850910)
XLA Ops:
  0.6 48.7 %shard_map.104 = (f32[8,128,512]{2,1,0:T(8,128)}, f32[1,256]{1,0:T(1,128)}) custom-call(f32[8,128,512]{2,1,0:T(8,128)} %control.1, bf16[8,128,512]{2,1,0:T(8,128)(2,1)} %scale.1, f32[8,128]{1,0:T(8,128)} %rate_x_h.1, f32[8,1024]{1,0:T(8,128)} %rate_y_h.1, s32[1,256]{1,0:T(1,128)} %bitcast.6, s32[16,256]{1,0:T(8,128)} %bitcast.5, f32[256,128]{1,0:T(8,128)} %weights_h.1, ...), custom_call_target="tpu_custom_call" | custom-call | tf_op jit(solution)/shard_map/pallas_call | solution.py:611
  49.3 0.0 copy-start
  49.3 3.1 %copy.13 = f32[8,128,512]{2,1,0:T(8,128)} copy(f32[8,128,512]{2,1,0:T(8,128)} %get-tuple-element.8) | data formatting | bytes 4194304
  52.4 0.0 copy-done
  52.4 0.6 %copy.14 = f32[256]{0:T(256)} copy(f32[256]{0:T(256)S(1)} %bitcast.9) | data formatting | bytes 2048
Async XLA Ops:
  49.3 3.1 %copy-start = (f32[1,256]{1,0:T(1,128)S(1)}, f32[1,256]{1,0:T(1,128)}, u32[]{:S(2)}) copy-start(f32[1,256]{1,0:T(1,128)} %get-tuple-element.5) | copy-start | bytes 3076
